TPU v7x, 128 devices: a whole 4x4x4 slice. The times are simulated.
128 devices in a mesh: section: 2 (over x_lo), rows: 8 (over y, x_hi), chan: 8 (over z, core).
Axes of the slice: x: 4 (x_hi: 2, x_lo: 2; x = x_hi * 2 + x_lo), y: 4, z: 4, core: 2. Of those that a mesh axis runs over, the one named last changes fastest.
Arguments:
- condition: float32 [12, 128, 1024], P(None, 'rows'), may hold values from -6 to 6
- target: float32 [12, 128, 1024], P(None, 'rows'), may hold values from -6 to 6
- noise_draw: float32 [12, 128, 1024], P(None, 'rows'), may hold values from -6 to 6
- sigma_index: int32 [1], replicated, may hold values from 0 to 31
- reg_first: bfloat16 [3, 3, 12, 128], P(None, None, None, 'chan'), may hold values from -0.625 to 0.625
- reg_second: bfloat16 [3, 3, 128, 12], P(None, None, 'chan'), may hold values from -0.1875 to 0.1875
- first_kernel: bfloat16 [3, 3, 24, 128], P(None, None, None, ('section', 'chan')), may hold values from -0.4375 to 0.4375
- second_kernel: bfloat16 [3, 3, 128, 128], P(None, None, None, ('section', 'chan')), may hold values from -0.1875 to 0.1875
- third_kernel: bfloat16 [3, 3, 128, 12], P(None, None, ('section', 'chan')), may hold values from -0.1875 to 0.1875
- film_scale: bfloat16 [128], P(('section', 'chan')), may hold values from -4 to 4
Outputs:
- denoised: bfloat16 [12, 128, 1024], P(None, 'rows')
- grad_first: float32 [3, 3, 24, 128], P(None, None, None, ('section', 'chan'))
- grad_second: float32 [3, 3, 128, 128], P(None, None, None, ('section', 'chan'))
- grad_third: float32 [3, 3, 128, 12], P(None, None, ('section', 'chan'))
- grad_film: float32 [128], P(('section', 'chan'))
Inputs may be any that keep to these rules, and one draw needn't show every extreme that they name: `sigma_index`: an index into the table of 32 noise levels.
All inputs are finite; a program needn't handle non-finite values.
Results may differ from a plain program's by a relative error of at most 0.008.
Values may be sent and summed in bfloat16 or wider, within the bound.
No kernel may reach another device: no remote copies, remote signals or barrier semaphores. Data moves between devices by JAX's collectives and lax.ppermute only.
A program may use at most 128 MiB of HBM per device.

v0:
```python
import math
import jax
import jax.numpy as jnp
from jax import lax
from jax.sharding import PartitionSpec as P

COUT = 12
NSIG = 32
sigma_low = 0.25
sigma_high = 4.0
rho_power = 7.0
sigma_data = 0.5


def padded(array, sides, width):
    for axis, dim in sides:
        size, length = (lax.axis_size(axis), array.shape[dim])
        up = [(i, (i + 1) % size) for i in range(size - 1)]
        down = [(j, i) for i, j in up]
        last = lax.slice_in_dim(array, length - width, length, axis=dim)
        leading = lax.slice_in_dim(array, 0, width, axis=dim)
        before = lax.ppermute(last, axis, up)
        after = lax.ppermute(leading, axis, down)
        array = jnp.concatenate([before, array, after], axis=dim)
    return array


def noise_terms(sigma_index):
    steps_at = jnp.arange(NSIG, dtype=jnp.float32) / (NSIG - 1)
    high_root = sigma_high ** (1.0 / rho_power)
    low_root = sigma_low ** (1.0 / rho_power)
    levels = (high_root + steps_at * (low_root - high_root)) ** rho_power
    picked = jnp.arange(NSIG, dtype=jnp.int32) == sigma_index[0]
    sigma_level = jnp.sum(jnp.where(picked, levels, jnp.zeros_like(levels)))
    total_var = sigma_level * sigma_level + sigma_data * sigma_data
    skip_coef = sigma_data * sigma_data / total_var
    out_coef = sigma_level * sigma_data / jnp.sqrt(total_var)
    in_coef = 1.0 / jnp.sqrt(total_var)
    noise_coef = jnp.log(8.0 * sigma_level) / 4.0
    loss_weight = total_var / (sigma_level * sigma_data) ** 2
    return (sigma_level, skip_coef, out_coef, in_coef, noise_coef, loss_weight)


def conv_rows(grid_field, kernel):
    result_conv = lax.conv_general_dilated(
        grid_field[None],
        kernel,
        (1, 1),
        ((0, 0), (1, 1)),
        dimension_numbers=("NCHW", "HWIO", "NCHW"),
        preferred_element_type=jnp.float32,
    )
    return result_conv[0]


def kernel_grad(grid_field, delta_in):
    result_conv = lax.conv_general_dilated(
        grid_field[:, None],
        delta_in[:, None],
        (1, 1),
        ((0, 0), (1, 1)),
        dimension_numbers=("NCHW", "OIHW", "NCHW"),
        preferred_element_type=jnp.float32,
    )
    return jnp.transpose(result_conv, (2, 3, 0, 1))


def turned(kernel):
    return jnp.transpose(jnp.flip(kernel, (0, 1)), (0, 1, 3, 2))


def silu_slope(pre_act):
    sigmoid_at = jax.nn.sigmoid(pre_act)
    return sigmoid_at * (1.0 + pre_act * (1.0 - sigmoid_at))


def grid_rows(grid_field, first_row, total_rows):
    places = first_row + jnp.arange(grid_field.shape[1], dtype=jnp.int32)
    inside = (places >= 0) & (places < total_rows)
    return jnp.where(inside[None, :, None], grid_field, jnp.zeros_like(grid_field))


def shards(
    condition,
    target,
    noise_draw,
    sigma_index,
    reg_first,
    reg_second,
    first_kernel,
    second_kernel,
    third_kernel,
    film_scale,
):
    rows_dev = condition.shape[1]
    grid_width = condition.shape[2]
    total_rows = rows_dev * lax.axis_size("rows")
    slab_start = lax.axis_index("rows") * rows_dev
    section_id = lax.axis_index("section")
    member = lax.axis_index(("section", "chan"))
    local_ch = film_scale.shape[0]
    sigma_level, skip_coef, out_coef, in_coef, noise_coef, loss_weight = noise_terms(sigma_index)
    grad_scale = 1.0 / math.sqrt(COUT * total_rows * grid_width)
    cond_low = condition.astype(jnp.bfloat16)
    cond_rim = padded(cond_low, (("rows", 1),), 2)
    half_rows = rows_dev // lax.axis_size("section")
    half_start = section_id * half_rows
    reg_input = lax.dynamic_slice_in_dim(cond_rim, half_start, half_rows + 4, 1)
    reg_hidden = jax.nn.silu(conv_rows(reg_input, reg_first))
    reg_hidden = grid_rows(reg_hidden, slab_start + half_start - 1, total_rows).astype(jnp.bfloat16)
    mean_part = conv_rows(reg_hidden, reg_second)
    mean_half = lax.psum(mean_part, "chan").astype(jnp.bfloat16)
    mean_field = lax.all_gather(mean_half, "section", axis=1, tiled=True)
    resid_field = target - mean_field.astype(jnp.float32)
    noisy_field = resid_field + sigma_level * noise_draw
    scaled_in = (in_coef * noisy_field).astype(jnp.bfloat16)
    film_gain = 1.0 + noise_coef * film_scale.astype(jnp.float32)
    input_rim = padded(scaled_in, (("rows", 1),), 2)
    stacked = jnp.concatenate([input_rim, cond_rim], 0)
    whole_first, whole_film = (
        lax.all_gather(first_kernel, ("section", "chan"), axis=3, tiled=True),
        lax.all_gather(film_scale, ("section", "chan"), axis=0, tiled=True),
    )
    first_all = conv_rows(stacked, whole_first)
    gain_all = (1.0 + noise_coef * whole_film.astype(jnp.float32))[:, None, None]
    hidden_full = grid_rows(jax.nn.silu(first_all * gain_all), slab_start - 1, total_rows).astype(
        jnp.bfloat16
    )
    first_mine = lax.dynamic_slice_in_dim(first_all, member * local_ch, local_ch, 0)[:, 1:-1]
    second_act = conv_rows(hidden_full, second_kernel)
    second_hidden = jax.nn.silu(second_act).astype(jnp.bfloat16)
    second_rim = padded(second_hidden, (("rows", 1),), 1)
    out_part = conv_rows(second_rim, third_kernel)
    out_full = lax.psum(out_part, ("section", "chan"))
    den_value = skip_coef * noisy_field + out_coef * out_full
    out_delta = (2.0 * loss_weight * out_coef * grad_scale * (den_value - resid_field)).astype(
        jnp.bfloat16
    )
    out_delta_rim = padded(out_delta, (("rows", 1),), 1)
    grad_third = kernel_grad(second_rim, out_delta)
    second_delta = (conv_rows(out_delta_rim, turned(third_kernel)) * silu_slope(second_act)).astype(
        jnp.bfloat16
    )
    second_delta_rim = padded(second_delta, (("rows", 1),), 1)
    grad_second = kernel_grad(hidden_full, second_delta)
    whole_second = lax.all_gather(second_kernel, ("section", "chan"), axis=3, tiled=True)
    mine_second = turned(lax.dynamic_slice_in_dim(whole_second, member * local_ch, local_ch, 2))
    empty_sum = jnp.zeros((local_ch, rows_dev, grid_width), jnp.float32)
    shard_part = lax.all_gather(second_delta_rim, ("section", "chan"), axis=0, tiled=True)
    kernel_part = lax.slice_in_dim(mine_second, 0, shard_part.shape[0], axis=2)
    back_first = empty_sum + conv_rows(shard_part, kernel_part)
    gain_mine = film_gain[:, None, None]
    first_grad = back_first * silu_slope(first_mine * gain_mine)
    grad_film = noise_coef * jnp.sum(first_grad * first_mine, axis=(1, 2))
    first_delta = (first_grad * gain_mine).astype(jnp.bfloat16)
    grad_first = kernel_grad(stacked[:, 1:-1], first_delta)
    grad_parts = (grad_first, grad_second, grad_third, grad_film)
    den_out = den_value.astype(jnp.bfloat16)
    grad_first, grad_second, grad_third, grad_film = lax.psum(
        (grad_parts[0], grad_parts[1], grad_parts[2], grad_parts[3]), "rows"
    )
    return (den_out, grad_first, grad_second, grad_third, grad_film)


def solution(mesh):
    return jax.shard_map(
        shards,
        mesh=mesh,
        in_specs=(
            P(None, "rows", None),
            P(None, "rows", None),
            P(None, "rows", None),
            P(),
            P(None, None, None, "chan"),
            P(None, None, "chan", None),
            P(None, None, None, ("section", "chan")),
            P(None, None, None, ("section", "chan")),
            P(None, None, ("section", "chan"), None),
            P(("section", "chan")),
        ),
        out_specs=(
            P(None, "rows", None),
            P(None, None, None, ("section", "chan")),
            P(None, None, None, ("section", "chan")),
            P(None, None, ("section", "chan"), None),
            P(("section", "chan")),
        ),
        check_vma=False,
    )
```

profile of v0, /device:TPU:0, one launch (start us, length us, event | category | flops | bytes accessed | tf_op | source)
XLA Modules:
  0.0 844.1 jit_solution(11145103124998721474)
XLA Ops:
  18.9 30.4 %all-reduce = bf16[128]{0:T(256)(128)(2,1)S(1)} all-reduce(bf16[128]{0:T(256)(128)(2,1)S(1)} %dynamic-update-slice), channel_id=1, replica_groups=mesh['section'=2,'rows'=8,'chan'=8] {'section','chan'}, use_global_device_ids=true, to_apply=%add | all-reduce | flops 128 | bytes 512
  75.3 27.6 %all-reduce.6 = bf16[12,8,1024]{2,1,0:T(8,128)(2,1)S(1)} all-reduce(f32[12,8,1024]{2,1,0:T(8,128)S(1)} %slice_bitcast_fusion.3), channel_id=1, replica_groups=mesh['section'=2,'rows'=8,'chan'=8] {'chan'}, use_global_device_ids=true, to_apply=%region_1.2 | all-reduce | flops 98304 | bytes 589824 | tf_op jit(solution)/shard_map/psum | solution.py:112
  119.8 18.4 %all_gather.16 = bf16[3,3,24,128]{2,3,1,0:T(8,128)(2,1)S(1)} all-gather(bf16[3,3,24,8]{2,3,1,0:T(8,128)(2,1)S(1)} %copy-done.8), channel_id=1, replica_groups=mesh['section'=2,'rows'=8,'chan'=8] {'section','chan'}, dimensions={3}, use_global_device_ids=true | all-gather | bytes 58752 | tf_op jit(solution)/shard_map/all_gather | solution.py:121
  163.7 12.6 %fusion.30 = f32[16,8,129,8]{3,1,2,0:T(8,128)} fusion(bf16[3,3,128,8]{2,3,1,0:T(8,128)(2,1)S(1)} %copy-done.9, bf16[18,1,7,1,128]{4,2,3,0,1:T(8,128)(2,1)S(1)} %get-tuple-element.17, bf16[18,1,7,1,128]{4,2,3,0,1:T(8,128)(2,1)S(1)} %get-tuple-element.16, bf16[18,1,8,129,128]{4,2,3,0,1:T(8,128)(2,1)S(1)} %select_bitcast_fusion), kind=kOutput, calls=%fused_computation.39 | convolution fusion | flops 328495104 | bytes 5366784 | tf_op jit(solution)/shard_map/conv_general_dilated | solution.py:45
  192.3 18.4 %all_gather.19 = bf16[3,3,128,128]{2,3,1,0:T(8,128)(2,1)} all-gather(bf16[3,3,128,8]{2,3,1,0:T(8,128)(2,1)S(1)} %copy-done.9), channel_id=1, replica_groups=mesh['section'=2,'rows'=8,'chan'=8] {'section','chan'}, dimensions={3}, use_global_device_ids=true | all-gather | bytes 313344 | tf_op jit(solution)/shard_map/all_gather | solution.py:146
  211.5 18.9 %copy.120 = f32[18,8,129,128]{2,1,3,0:T(8,128)} copy(f32[18,8,129,128]{3,1,2,0:T(8,128)} %copy-done.2) | data formatting | bytes 19021824 | tf_op jit(solution)/shard_map/conv_general_dilated | solution.py:45
  230.4 17.9 %reshape.184 = f32[18,1,1032,128]{2,3,0,1:T(8,128)} reshape(f32[18,8,129,128]{2,1,3,0:T(8,128)} %copy.120) | data formatting | bytes 19021824 | tf_op jit(solution)/shard_map/conv_general_dilated | solution.py:45
  255.9 11.2 %broadcast_select_fusion.3 = f32[16,8,129,12]{3,1,2,0:T(8,128)} fusion(pred[8,129]{0,1:T(8,128)(4,1)S(1)} %copy-done.10, bf16[3,3,8,12]{3,2,1,0:T(8,128)(2,1)S(1)} %copy-done.13, bf16[8,18,1,7,2]{0,3,4,1,2:T(8,128)(2,1)S(1)} %slice.77, bf16[8,18,1,8,129]{0,3,4,1,2:T(8,128)(2,1)} %copy.95), kind=kOutput, calls=%fused_computation.59 | convolution fusion | flops 29636352 | bytes 1096584 | tf_op jit(solution)/shard_map/conv_general_dilated | solution.py:45
  287.3 111.4 %all-reduce.5.cloned.1.call-done = f32[12,16,1024]{2,1,0:T(8,128)} async-done(((f32[12,16,1024]{2,1,0:T(8,128)}), f32[12,16,1024]{2,1,0:T(8,128)}) %all-reduce.5.cloned.1.call-update) | async-done | bytes 786448 | tf_op jit(solution)/shard_map/psum | solution.py:134
  410.0 9.3 %slice.88 = f32[18,1,1024,128]{2,3,0,1:T(8,128)} slice(f32[18,1,1032,128]{2,3,0,1:T(8,128)} %reshape.184), slice={[0:18], [0:1], [0:1024], [0:128]} | slice | bytes 18874368 | tf_op jit(solution)/shard_map/conv_general_dilated | solution.py:45
  429.1 11.0 %broadcast_select_fusion.2 = f32[16,8,129,8]{3,1,2,0:T(8,128)} fusion(pred[8,129]{0,1:T(8,128)(4,1)S(1)} %copy-done.10, bf16[3,3,8,12]{3,2,1,0:T(8,128)(2,1)S(1)} %copy-done.13, bf16[12,18,1,7,2]{0,3,4,1,2:T(8,128)(2,1)S(1)} %slice.82, bf16[12,18,1,8,129]{0,3,4,1,2:T(8,128)(2,1)} %copy.99), kind=kOutput, calls=%fused_computation.58 | convolution fusion | flops 30023040 | bytes 983016 | tf_op jit(solution)/shard_map/conv_general_dilated | solution.py:45
  458.8 13.2 %copy.108 = bf16[24,1,18,1024]{0,1,3,2:T(2,128)(2,1)} copy(bf16[24,1,18,1024]{3,2,0,1:T(8,128)(2,1)S(1)} %slice_bitcast_fusion) | data formatting | bytes 1769472 | tf_op jit(solution)/shard_map/broadcast_in_dim | solution.py:58
  472.1 21.3 %copy.110 = bf16[128,1,18,1024]{0,1,3,2:T(2,128)(2,1)} copy(bf16[128,1,18,1024]{3,0,2,1:T(8,128)(2,1)} %select_convert_fusion.1) | data formatting | bytes 9437184 | tf_op jit(solution)/shard_map/convert_element_type | solution.py:126
  493.4 15.4 %copy.112 = bf16[8,1,18,1024]{0,1,3,2:T(2,128)(2,1)} copy(bf16[8,1,18,1024]{3,0,2,1:T(8,128)(2,1)S(1)} %copy-done.6) | data formatting | bytes 589824 | tf_op jit(solution)/shard_map/broadcast_in_dim | solution.py:58
  508.8 9.0 %copy.113 = bf16[12,1,16,1024]{0,1,3,2:T(2,128)(2,1)} copy(bf16[12,1,16,1024]{3,2,0,1:T(8,128)(2,1)S(1)} %bitcast.183) | data formatting | bytes 786432 | tf_op jit(solution)/shard_map/broadcast_in_dim | solution.py:59
  518.6 52.5 %fusion.140 = f32[3,3,8,12]{3,2,1,0:T(8,128)S(1)} fusion(bf16[8,1,18,1024]{0,1,3,2:T(2,128)(2,1)} %copy.112, bf16[12,1,16,1024]{0,1,3,2:T(2,128)(2,1)} %copy.113), kind=kOutput, calls=%fused_computation.171 | convolution fusion | flops 28293120 | bytes 691584 | tf_op jit(solution)/shard_map/transpose | solution.py:65
  571.3 14.2 %copy.111 = bf16[8,1,16,1024]{0,1,3,2:T(2,128)(2,1)} copy(bf16[8,1,16,1024]{3,0,2,1:T(8,128)(2,1)S(1)} %fusion.84) | data formatting | bytes 524288 | tf_op jit(solution)/shard_map/convert_element_type | solution.py:141
  585.5 66.0 %fusion.139 = f32[3,3,128,8]{2,3,1,0:T(8,128)S(1)} fusion(bf16[128,1,18,1024]{0,1,3,2:T(2,128)(2,1)} %copy.110, bf16[8,1,16,1024]{0,1,3,2:T(2,128)(2,1)} %copy.111), kind=kOutput, calls=%fused_computation.170 | convolution fusion | flops 301793280 | bytes 5017600 | tf_op jit(solution)/shard_map/transpose | solution.py:65
  659.1 17.5 %reshape.183 = bf16[128,18,1,8,129]{4,3,0,1,2:T(8,128)(2,1)} reshape(bf16[128,18,1,1032]{3,0,1,2:T(8,128)(2,1)} %pad.12) | data formatting | bytes 9510912 | tf_op jit(solution)/shard_map/conv_general_dilated | solution.py:45
  676.6 13.1 %copy.103 = bf16[128,18,1,8,129]{0,3,4,1,2:T(8,128)(2,1)} copy(bf16[128,18,1,8,129]{4,3,0,1,2:T(8,128)(2,1)} %reshape.183) | data formatting | bytes 9510912 | tf_op jit(solution)/shard_map/conv_general_dilated | solution.py:45
  690.7 14.4 %broadcast_select_fusion.1 = f32[16,8,129,8]{3,1,2,0:T(8,128)} fusion(pred[8,129]{0,1:T(8,128)(4,1)S(1)} %copy-done.10, bf16[128,18,1,7,2]{0,3,4,1,2:T(8,128)(2,1)S(1)} %slice.86, bf16[128,18,1,8,129]{0,3,4,1,2:T(8,128)(2,1)} %copy.103, bf16[3,3,128,128]{2,3,1,0:T(8,128)(2,1)S(1)} %copy-done.7, s32[]{:T(128)S(6)} %select_n.34), kind=kOutput, calls=%fused_computation.57 | convolution fusion | flops 318968832 | bytes 5644300 | tf_op jit(solution)/shard_map/conv_general_dilated | solution.py:45
  712.9 14.2 %copy.109 = bf16[8,1,16,1024]{0,1,3,2:T(2,128)(2,1)} copy(bf16[8,1,16,1024]{3,0,2,1:T(8,128)(2,1)S(1)} %fusion.101) | data formatting | bytes 524288 | tf_op jit(solution)/shard_map/broadcast_in_dim | solution.py:59
  727.1 66.0 %fusion.138 = f32[3,3,24,8]{2,3,1,0:T(8,128)S(1)} fusion(bf16[24,1,18,1024]{0,1,3,2:T(2,128)(2,1)} %copy.108, bf16[8,1,16,1024]{0,1,3,2:T(2,128)(2,1)} %copy.109), kind=kOutput, calls=%fused_computation.169 | convolution fusion | flops 56586240 | bytes 1153792 | tf_op jit(solution)/shard_map/transpose | solution.py:65
  793.1 43.7 %all-reduce.1 = (f32[3,3,24,8]{2,3,1,0:T(8,128)}, f32[3,3,128,8]{2,3,1,0:T(8,128)}, f32[3,3,8,12]{3,2,1,0:T(8,128)}, f32[8]{0:T(128)}) all-reduce(f32[3,3,24,8]{2,3,1,0:T(8,128)S(1)} %fusion.138, f32[3,3,128,8]{2,3,1,0:T(8,128)S(1)} %fusion.139, ...), channel_id=1, replica_groups=mesh['section'=2,'rows'=8,'chan'=8] {'rows'}, use_global_device_ids=true, to_apply=%region_3.4 | all-reduce | flops 11816 | bytes 94528 | tf_op jit(solution)/shard_map/psum | solution.py:159
  (121 shorter events, 177.4 us)
Async XLA Ops:
  7.2 51.3 %copy-start = (bf16[3,3,12,16]{3,2,1,0:T(8,128)(2,1)S(1)}, bf16[3,3,12,16]{3,2,1,0:T(8,128)(2,1)}, u32[]{:S(2)}) copy-start(bf16[3,3,12,16]{3,2,1,0:T(8,128)(2,1)} %param.14) | copy-start | bytes 10372
  7.2 51.3 %copy-start.10 = (pred[8,129]{0,1:T(8,128)(4,1)S(1)}, pred[8,129]{0,1:T(8,128)(4,1)}, u32[]{:S(2)}) copy-start(pred[8,129]{0,1:T(8,128)(4,1)} %constant.100) | copy-start | bytes 3100
  7.2 391.5 %all-reduce.5.cloned.1.call-start = ((), (), s32[]{:S(2)}) async-start(), calls=%async_computation | async-start | bytes 1572864 | tf_op jit(solution)/shard_map/psum | solution.py:134
  8.5 44.0 %collective-permute-start = (bf16[12,2,1024]{2,1,0:T(2,128)(2,1)S(1)}, bf16[12,2,1024]{2,1,0:T(2,128)(2,1)S(1)}, u32[]{:S(2)}, u32[]{:S(2)}) collective-permute-start(bf16[12,2,1024]{2,1,0:T(2,128)(2,1)S(1)} %get-tuple-element.26), channel_id=1, source_target_pairs={{0,8},{8,16},{16,24},{24,32},{32,40},{40,48},{48,56},{1,9},{9,17},... | collective-permute-start | bytes 147464 | tf_op jit(solution)/shard_map/ppermute | solution.py:22
  13.5 39.0 %collective-permute-start.1 = (bf16[12,2,1024]{2,1,0:T(2,128)(2,1)S(1)}, bf16[12,2,1024]{2,1,0:T(2,128)(2,1)S(1)}, u32[]{:S(2)}, u32[]{:S(2)}) collective-permute-start(bf16[12,2,1024]{2,1,0:T(2,128)(2,1)S(1)} %get-tuple-element.27), channel_id=1, source_target_pairs={{8,0},{16,8},{24,16},{32,24},{40,32},{48,40},{56,48},{9,1},{17,9},... | collective-permute-start | bytes 147464 | tf_op jit(solution)/shard_map/ppermute | solution.py:23
  58.5 7.4 copy-start.12
  70.7 38.6 %copy-start.4 = (f32[12,16,1024]{2,1,0:T(8,128)S(1)}, f32[12,16,1024]{2,1,0:T(8,128)}, u32[]{:S(2)}) copy-start(f32[12,16,1024]{2,1,0:T(8,128)} %param.11) | copy-start | bytes 2359300
  70.7 49.0 %copy-start.8 = (bf16[3,3,24,8]{2,3,1,0:T(8,128)(2,1)S(1)}, bf16[3,3,24,8]{2,3,1,0:T(8,128)(2,1)}, u32[]{:S(2)}) copy-start(bf16[3,3,24,8]{2,3,1,0:T(8,128)(2,1)} %param.16) | copy-start | bytes 10372
  109.3 28.8 %copy-start.3 = (bf16[12,16,1024]{2,1,0:T(8,128)(2,1)}, bf16[12,16,1024]{2,1,0:T(8,128)(2,1)S(1)}, u32[]{:S(2)}) copy-start(bf16[12,16,1024]{2,1,0:T(8,128)(2,1)S(1)} %all_gather.15) | copy-start | bytes 1179652
  111.4 26.7 %collective-permute-start.3 = (bf16[12,2,1024]{2,1,0:T(2,128)(2,1)S(1)}, bf16[12,2,1024]{2,1,0:T(2,128)(2,1)S(1)}, u32[]{:S(2)}, u32[]{:S(2)}) collective-permute-start(bf16[12,2,1024]{2,1,0:T(2,128)(2,1)S(1)} %get-tuple-element.25), channel_id=1, source_target_pairs={{8,0},{16,8},{24,16},{32,24},{40,32},{48,40},{56,48},{9,1},{17,9},... | collective-permute-start | bytes 147464 | tf_op jit(solution)/shard_map/ppermute | solution.py:23
  112.7 25.4 %collective-permute-start.2 = (bf16[12,2,1024]{2,1,0:T(2,128)(2,1)S(1)}, bf16[12,2,1024]{2,1,0:T(2,128)(2,1)S(1)}, u32[]{:S(2)}, u32[]{:S(2)}) collective-permute-start(bf16[12,2,1024]{2,1,0:T(2,128)(2,1)S(1)} %get-tuple-element.24), channel_id=1, source_target_pairs={{0,8},{8,16},{16,24},{24,32},{32,40},{40,48},{48,56},{1,9},{9,17},... | collective-permute-start | bytes 147464 | tf_op jit(solution)/shard_map/ppermute | solution.py:22
  183.7 64.6 %collective-permute-start.5 = (bf16[8,1,1024]{2,0,1:T(8,128)(2,1)S(1)}, bf16[8,1,1024]{2,0,1:T(8,128)(2,1)S(1)}, u32[]{:S(2)}, u32[]{:S(2)}) collective-permute-start(bf16[8,1,1024]{2,0,1:T(8,128)(2,1)S(1)} %get-tuple-element.33), channel_id=1, source_target_pairs={{8,0},{16,8},{24,16},{32,24},{40,32},{48,40},{56,48},{9,1},{17,9},... | collective-permute-start | bytes 49160 | tf_op jit(solution)/shard_map/ppermute | solution.py:23
  185.0 63.3 %collective-permute-start.4 = (bf16[8,1,1024]{2,0,1:T(8,128)(2,1)S(1)}, bf16[8,1,1024]{2,0,1:T(8,128)(2,1)S(1)}, u32[]{:S(2)}, u32[]{:S(2)}) collective-permute-start(bf16[8,1,1024]{2,0,1:T(8,128)(2,1)S(1)} %get-tuple-element.32), channel_id=1, source_target_pairs={{0,8},{8,16},{16,24},{24,32},{32,40},{40,48},{48,56},{1,9},{9,17},... | collective-permute-start | bytes 49160 | tf_op jit(solution)/shard_map/ppermute | solution.py:22
  248.3 7.5 copy-start.13
  278.1 373.3 %all-gather.2.cloned.1.call-start = ((), (), s32[]{:S(2)}) async-start(), calls=%async_computation.1 | async-start | bytes 5013504 | tf_op jit(solution)/shard_map/all_gather | solution.py:149
  402.2 17.1 %collective-permute-start.7 = (bf16[12,1,1024]{2,1,0:T(2,128)(2,1)S(1)}, bf16[12,1,1024]{2,1,0:T(2,128)(2,1)S(1)}, u32[]{:S(2)}, u32[]{:S(2)}) collective-permute-start(bf16[12,1,1024]{2,1,0:T(2,128)(2,1)S(1)} %get-tuple-element.23), channel_id=1, source_target_pairs={{8,0},{16,8},{24,16},{32,24},{40,32},{48,40},{56,48},{9,1},{17,9},... | collective-permute-start | bytes 73736 | tf_op jit(solution)/shard_map/ppermute | solution.py:23
  403.5 15.8 %collective-permute-start.6 = (bf16[12,1,1024]{2,1,0:T(2,128)(2,1)S(1)}, bf16[12,1,1024]{2,1,0:T(2,128)(2,1)S(1)}, u32[]{:S(2)}, u32[]{:S(2)}) collective-permute-start(bf16[12,1,1024]{2,1,0:T(2,128)(2,1)S(1)} %get-tuple-element.22), channel_id=1, source_target_pairs={{0,8},{8,16},{16,24},{24,32},{32,40},{40,48},{48,56},{1,9},{9,17},... | collective-permute-start | bytes 73736 | tf_op jit(solution)/shard_map/ppermute | solution.py:22
  449.4 68.4 %collective-permute-start.9 = (bf16[8,1,1024]{2,0,1:T(8,128)(2,1)S(1)}, bf16[8,1,1024]{2,0,1:T(8,128)(2,1)S(1)}, u32[]{:S(2)}, u32[]{:S(2)}) collective-permute-start(bf16[8,1,1024]{2,0,1:T(8,128)(2,1)S(1)} %get-tuple-element.31), channel_id=1, source_target_pairs={{8,0},{16,8},{24,16},{32,24},{40,32},{48,40},{56,48},{9,1},{17,9},... | collective-permute-start | bytes 49160 | tf_op jit(solution)/shard_map/ppermute | solution.py:23
  450.7 67.1 %collective-permute-start.8 = (bf16[8,1,1024]{2,0,1:T(8,128)(2,1)S(1)}, bf16[8,1,1024]{2,0,1:T(8,128)(2,1)S(1)}, u32[]{:S(2)}, u32[]{:S(2)}) collective-permute-start(bf16[8,1,1024]{2,0,1:T(8,128)(2,1)S(1)} %get-tuple-element.30), channel_id=1, source_target_pairs={{0,8},{8,16},{16,24},{24,32},{32,40},{40,48},{48,56},{1,9},{9,17},... | collective-permute-start | bytes 49160 | tf_op jit(solution)/shard_map/ppermute | solution.py:22
  472.1 21.3 %copy-start.6 = (bf16[8,1,18,1024]{3,0,2,1:T(8,128)(2,1)S(1)}, bf16[8,1,18,1024]{3,0,2,1:T(8,128)(2,1)}, u32[]{:S(2)}) copy-start(bf16[8,1,18,1024]{3,0,2,1:T(8,128)(2,1)} %get-tuple-element.28) | copy-start | bytes 884740
  676.6 14.1 %copy-start.7 = (bf16[3,3,128,128]{2,3,1,0:T(8,128)(2,1)S(1)}, bf16[3,3,128,128]{2,3,1,0:T(8,128)(2,1)}, u32[]{:S(2)}) copy-start(bf16[3,3,128,128]{2,3,1,0:T(8,128)(2,1)} %all_gather.19) | copy-start | bytes 884740
  705.0 7.3 copy-start.5
  705.0 7.3 copy-start.11
  727.1 109.7 %copy-start.1 = (bf16[3,3,12,16]{3,2,1,0:T(8,128)(2,1)S(1)}, bf16[3,3,12,16]{3,2,1,0:T(8,128)(2,1)}, u32[]{:S(2)}) copy-start(bf16[3,3,12,16]{3,2,1,0:T(8,128)(2,1)} %param.14) | copy-start | bytes 10372
  (2 other events, 7.8 us)
Sparse Core Ops, SparseCore 0:
  278.3 120.3 all-reduce.4
  518.7 40.0 all-gather.1
where the time goes:
time: 855 us; the launch traced here: 844 us
  matrix products  255 us (30%)
  local copies, waits for them, and re-layouts  251 us (29%)
  blocking collectives  145 us (17%)
  waiting for transfers between devices  111 us (13%)
  starting transfers between devices  38 us (4%)
  other arithmetic  25.3 us (3%)
  between operations  19.2 us (2%)
    transpose x3, matrix products, kernel_grad(): return jnp.transpose(result_conv, (2, 3, 0, 1))  184 us
    conv_general_dilated x28, local copies, waits for them, and re-layouts, conv_rows(): lax.conv_general_dilated(grid_field[None], kernel, (1, 1), ((0, 0), (1, 1...  147 us
    psum x1, waiting for transfers between devices, shards(): out_full = lax.psum(out_part, ('section', 'chan'))  111 us
    conv_general_dilated x7, matrix products, conv_rows(): lax.conv_general_dilated(grid_field[None], kernel, (1, 1), ((0, 0), (1, 1...  70.3 us
    psum x1, blocking collectives, shards(): lax.psum((grad_parts[0], grad_parts[1], grad_parts[2], grad_parts[3]), 'r...  43.7 us
    ppermute x5, starting transfers between devices, padded(): before = lax.ppermute(last, axis, up)  31.5 us
    unnamed x1, blocking collectives  30.4 us
    broadcast_in_dim x3, local copies, waits for them, and re-layouts, kernel_grad(): grid_field[:, None]  29 us
  transfers between devices with their start and end apart: 12, of which 1 were waited for; matrix products, arithmetic and copies ran while one was open for 30% of the time, Pallas kernels for 0%

commit v1 on v0

--- a/solution.py
+++ b/solution.py
@@ -131,7 +131,7 @@
     second_hidden = jax.nn.silu(second_act).astype(jnp.bfloat16)
     second_rim = padded(second_hidden, (("rows", 1),), 1)
     out_part = conv_rows(second_rim, third_kernel)
-    out_full = lax.psum(out_part, ("section", "chan"))
+    out_full = lax.psum(lax.psum(out_part, "section"), "chan")
     den_value = skip_coef * noisy_field + out_coef * out_full
     out_delta = (2.0 * loss_weight * out_coef * grad_scale * (den_value - resid_field)).astype(
         jnp.bfloat16

time: 855 us -> 802 us (0.938)
  waiting for transfers between devices: 111 us -> 57.2 us
    psum x1 -> x2, waiting for transfers between devices: 111 us -> 55.7 us  [shards(): out_full = lax.psum(lax.psum(out_part, 'section'), 'chan')]
  transfers between devices with their start and end apart: 12 -> 13, of which waited for: 1 -> 2; matrix products, arithmetic and copies ran while one was open for 30% -> 32% of each run, Pallas kernels for 0% -> 0%
where the time goes in v1:
time: 802 us; the launch traced here: 791 us
  matrix products  255 us (32%)
  local copies, waits for them, and re-layouts  251 us (31%)
  blocking collectives  145 us (18%)
  waiting for transfers between devices  57.2 us (7%)
  starting transfers between devices  38.8 us (5%)
  other arithmetic  24.4 us (3%)
  between operations  18.9 us (2%)
    transpose x3, matrix products, kernel_grad(): return jnp.transpose(result_conv, (2, 3, 0, 1))  184 us
    conv_general_dilated x28, local copies, waits for them, and re-layouts, conv_rows(): lax.conv_general_dilated(grid_field[None], kernel, (1, 1), ((0, 0), (1, 1...  147 us
    conv_general_dilated x7, matrix products, conv_rows(): lax.conv_general_dilated(grid_field[None], kernel, (1, 1), ((0, 0), (1, 1...  70.5 us
    psum x2, waiting for transfers between devices, shards(): out_full = lax.psum(lax.psum(out_part, 'section'), 'chan')  55.7 us
    psum x1, blocking collectives, shards(): lax.psum((grad_parts[0], grad_parts[1], grad_parts[2], grad_parts[3]), 'r...  43.9 us
    ppermute x5, starting transfers between devices, padded(): before = lax.ppermute(last, axis, up)  32.2 us
    unnamed x1, blocking collectives  30.4 us
    broadcast_in_dim x3, local copies, waits for them, and re-layouts, kernel_grad(): grid_field[:, None]  29 us
  transfers between devices with their start and end apart: 13, of which 2 were waited for; matrix products, arithmetic and copies ran while one was open for 32% of the time, Pallas kernels for 0%

profile of v1, /device:TPU:0, one launch (start us, length us, event | category | flops | bytes accessed | tf_op | source)
XLA Modules:
  0.0 791.0 jit_solution(14595186192358703844)
XLA Ops:
  18.9 30.4 %all-reduce = bf16[128]{0:T(256)(128)(2,1)S(1)} all-reduce(bf16[128]{0:T(256)(128)(2,1)S(1)} %dynamic-update-slice), channel_id=1, replica_groups=mesh['section'=2,'rows'=8,'chan'=8] {'section','chan'}, use_global_device_ids=true, to_apply=%add | all-reduce | flops 128 | bytes 512
  74.2 27.6 %all-reduce.9 = bf16[12,8,1024]{2,1,0:T(8,128)(2,1)S(1)} all-reduce(f32[12,8,1024]{2,1,0:T(8,128)S(1)} %slice_bitcast_fusion.3), channel_id=1, replica_groups=mesh['section'=2,'rows'=8,'chan'=8] {'chan'}, use_global_device_ids=true, to_apply=%region_1.2 | all-reduce | flops 98304 | bytes 589824 | tf_op jit(solution)/shard_map/psum | solution.py:112
  118.6 18.4 %all_gather.16 = bf16[3,3,24,128]{2,3,1,0:T(8,128)(2,1)S(1)} all-gather(bf16[3,3,24,8]{2,3,1,0:T(8,128)(2,1)S(1)} %copy-done.8), channel_id=1, replica_groups=mesh['section'=2,'rows'=8,'chan'=8] {'section','chan'}, dimensions={3}, use_global_device_ids=true | all-gather | bytes 58752 | tf_op jit(solution)/shard_map/all_gather | solution.py:121
  162.5 12.6 %fusion.30 = f32[16,8,129,8]{3,1,2,0:T(8,128)} fusion(bf16[3,3,128,8]{2,3,1,0:T(8,128)(2,1)S(1)} %copy-done.9, bf16[18,1,7,1,128]{4,2,3,0,1:T(8,128)(2,1)S(1)} %get-tuple-element.17, bf16[18,1,7,1,128]{4,2,3,0,1:T(8,128)(2,1)S(1)} %get-tuple-element.16, bf16[18,1,8,129,128]{4,2,3,0,1:T(8,128)(2,1)S(1)} %select_bitcast_fusion), kind=kOutput, calls=%fused_computation.39 | convolution fusion | flops 328495104 | bytes 5366784 | tf_op jit(solution)/shard_map/conv_general_dilated | solution.py:45
  200.4 11.2 %broadcast_select_fusion.3 = f32[16,8,129,12]{3,1,2,0:T(8,128)} fusion(pred[8,129]{0,1:T(8,128)(4,1)S(1)} %copy-done.10, bf16[3,3,8,12]{3,2,1,0:T(8,128)(2,1)S(1)} %copy-done.13, bf16[8,18,1,7,2]{0,3,4,1,2:T(8,128)(2,1)S(1)} %slice.77, bf16[8,18,1,8,129]{0,3,4,1,2:T(8,128)(2,1)} %copy.95), kind=kOutput, calls=%fused_computation.59 | convolution fusion | flops 29636352 | bytes 1096584 | tf_op jit(solution)/shard_map/conv_general_dilated | solution.py:45
  223.6 18.9 %all_gather.19 = bf16[3,3,128,128]{2,3,1,0:T(8,128)(2,1)} all-gather(bf16[3,3,128,8]{2,3,1,0:T(8,128)(2,1)S(1)} %copy-done.9), channel_id=1, replica_groups=mesh['section'=2,'rows'=8,'chan'=8] {'section','chan'}, dimensions={3}, use_global_device_ids=true | all-gather | bytes 313344 | tf_op jit(solution)/shard_map/all_gather | solution.py:146
  243.0 18.8 %copy.120 = f32[18,8,129,128]{2,1,3,0:T(8,128)} copy(f32[18,8,129,128]{3,1,2,0:T(8,128)} %copy-done.2) | data formatting | bytes 19021824 | tf_op jit(solution)/shard_map/conv_general_dilated | solution.py:45
  261.8 17.9 %reshape.184 = f32[18,1,1032,128]{2,3,0,1:T(8,128)} reshape(f32[18,8,129,128]{2,1,3,0:T(8,128)} %copy.120) | data formatting | bytes 19021824 | tf_op jit(solution)/shard_map/conv_general_dilated | solution.py:45
  288.6 55.7 %all-reduce.8.cloned.1.call-done = f32[12,16,1024]{2,1,0:T(8,128)} async-done(((f32[12,16,1024]{2,1,0:T(8,128)}), f32[12,16,1024]{2,1,0:T(8,128)}) %all-reduce.8.cloned.1.call-update) | async-done | bytes 786448 | tf_op jit(solution)/shard_map/psum | solution.py:134
  356.1 9.3 %slice.88 = f32[18,1,1024,128]{2,3,0,1:T(8,128)} slice(f32[18,1,1032,128]{2,3,0,1:T(8,128)} %reshape.184), slice={[0:18], [0:1], [0:1024], [0:128]} | slice | bytes 18874368 | tf_op jit(solution)/shard_map/conv_general_dilated | solution.py:45
  375.2 11.1 %broadcast_select_fusion.2 = f32[16,8,129,8]{3,1,2,0:T(8,128)} fusion(pred[8,129]{0,1:T(8,128)(4,1)S(1)} %copy-done.10, bf16[3,3,8,12]{3,2,1,0:T(8,128)(2,1)S(1)} %copy-done.13, bf16[12,18,1,7,2]{0,3,4,1,2:T(8,128)(2,1)S(1)} %slice.82, bf16[12,18,1,8,129]{0,3,4,1,2:T(8,128)(2,1)} %copy.99), kind=kOutput, calls=%fused_computation.58 | convolution fusion | flops 30023040 | bytes 983016 | tf_op jit(solution)/shard_map/conv_general_dilated | solution.py:45
  405.3 13.0 %copy.108 = bf16[24,1,18,1024]{0,1,3,2:T(2,128)(2,1)} copy(bf16[24,1,18,1024]{3,2,0,1:T(8,128)(2,1)S(1)} %slice_bitcast_fusion) | data formatting | bytes 1769472 | tf_op jit(solution)/shard_map/broadcast_in_dim | solution.py:58
  418.4 21.4 %copy.110 = bf16[128,1,18,1024]{0,1,3,2:T(2,128)(2,1)} copy(bf16[128,1,18,1024]{3,0,2,1:T(8,128)(2,1)} %select_convert_fusion.1) | data formatting | bytes 9437184 | tf_op jit(solution)/shard_map/convert_element_type | solution.py:126
  439.8 15.5 %copy.112 = bf16[8,1,18,1024]{0,1,3,2:T(2,128)(2,1)} copy(bf16[8,1,18,1024]{3,0,2,1:T(8,128)(2,1)S(1)} %copy-done.6) | data formatting | bytes 589824 | tf_op jit(solution)/shard_map/broadcast_in_dim | solution.py:58
  455.3 9.3 %copy.113 = bf16[12,1,16,1024]{0,1,3,2:T(2,128)(2,1)} copy(bf16[12,1,16,1024]{3,2,0,1:T(8,128)(2,1)S(1)} %bitcast.183) | data formatting | bytes 786432 | tf_op jit(solution)/shard_map/broadcast_in_dim | solution.py:59
  465.4 52.5 %fusion.140 = f32[3,3,8,12]{3,2,1,0:T(8,128)S(1)} fusion(bf16[8,1,18,1024]{0,1,3,2:T(2,128)(2,1)} %copy.112, bf16[12,1,16,1024]{0,1,3,2:T(2,128)(2,1)} %copy.113), kind=kOutput, calls=%fused_computation.171 | convolution fusion | flops 28293120 | bytes 691584 | tf_op jit(solution)/shard_map/transpose | solution.py:65
  518.1 14.3 %copy.111 = bf16[8,1,16,1024]{0,1,3,2:T(2,128)(2,1)} copy(bf16[8,1,16,1024]{3,0,2,1:T(8,128)(2,1)S(1)} %fusion.84) | data formatting | bytes 524288 | tf_op jit(solution)/shard_map/convert_element_type | solution.py:141
  532.4 66.0 %fusion.139 = f32[3,3,128,8]{2,3,1,0:T(8,128)S(1)} fusion(bf16[128,1,18,1024]{0,1,3,2:T(2,128)(2,1)} %copy.110, bf16[8,1,16,1024]{0,1,3,2:T(2,128)(2,1)} %copy.111), kind=kOutput, calls=%fused_computation.170 | convolution fusion | flops 301793280 | bytes 5017600 | tf_op jit(solution)/shard_map/transpose | solution.py:65
  606.0 17.5 %reshape.183 = bf16[128,18,1,8,129]{4,3,0,1,2:T(8,128)(2,1)} reshape(bf16[128,18,1,1032]{3,0,1,2:T(8,128)(2,1)} %pad.12) | data formatting | bytes 9510912 | tf_op jit(solution)/shard_map/conv_general_dilated | solution.py:45
  623.4 13.1 %copy.103 = bf16[128,18,1,8,129]{0,3,4,1,2:T(8,128)(2,1)} copy(bf16[128,18,1,8,129]{4,3,0,1,2:T(8,128)(2,1)} %reshape.183) | data formatting | bytes 9510912 | tf_op jit(solution)/shard_map/conv_general_dilated | solution.py:45
  637.5 14.4 %broadcast_select_fusion.1 = f32[16,8,129,8]{3,1,2,0:T(8,128)} fusion(pred[8,129]{0,1:T(8,128)(4,1)S(1)} %copy-done.10, bf16[128,18,1,7,2]{0,3,4,1,2:T(8,128)(2,1)S(1)} %slice.86, bf16[128,18,1,8,129]{0,3,4,1,2:T(8,128)(2,1)} %copy.103, bf16[3,3,128,128]{2,3,1,0:T(8,128)(2,1)S(1)} %copy-done.7, s32[]{:T(128)S(6)} %select_n.34), kind=kOutput, calls=%fused_computation.57 | convolution fusion | flops 318968832 | bytes 5644300 | tf_op jit(solution)/shard_map/conv_general_dilated | solution.py:45
  659.9 14.2 %copy.109 = bf16[8,1,16,1024]{0,1,3,2:T(2,128)(2,1)} copy(bf16[8,1,16,1024]{3,0,2,1:T(8,128)(2,1)S(1)} %fusion.101) | data formatting | bytes 524288 | tf_op jit(solution)/shard_map/broadcast_in_dim | solution.py:59
  674.1 66.0 %fusion.138 = f32[3,3,24,8]{2,3,1,0:T(8,128)S(1)} fusion(bf16[24,1,18,1024]{0,1,3,2:T(2,128)(2,1)} %copy.108, bf16[8,1,16,1024]{0,1,3,2:T(2,128)(2,1)} %copy.109), kind=kOutput, calls=%fused_computation.169 | convolution fusion | flops 56586240 | bytes 1153792 | tf_op jit(solution)/shard_map/transpose | solution.py:65
  740.1 43.9 %all-reduce.1 = (f32[3,3,24,8]{2,3,1,0:T(8,128)}, f32[3,3,128,8]{2,3,1,0:T(8,128)}, f32[3,3,8,12]{3,2,1,0:T(8,128)}, f32[8]{0:T(128)}) all-reduce(f32[3,3,24,8]{2,3,1,0:T(8,128)S(1)} %fusion.138, f32[3,3,128,8]{2,3,1,0:T(8,128)S(1)} %fusion.139, ...), channel_id=1, replica_groups=mesh['section'=2,'rows'=8,'chan'=8] {'rows'}, use_global_device_ids=true, to_apply=%region_4.5 | all-reduce | flops 11816 | bytes 94528 | tf_op jit(solution)/shard_map/psum | solution.py:159
  (126 shorter events, 179.0 us)
Async XLA Ops:
  7.2 50.1 %copy-start = (bf16[3,3,12,16]{3,2,1,0:T(8,128)(2,1)S(1)}, bf16[3,3,12,16]{3,2,1,0:T(8,128)(2,1)}, u32[]{:S(2)}) copy-start(bf16[3,3,12,16]{3,2,1,0:T(8,128)(2,1)} %param.14) | copy-start | bytes 10372
  7.2 50.1 %copy-start.10 = (pred[8,129]{0,1:T(8,128)(4,1)S(1)}, pred[8,129]{0,1:T(8,128)(4,1)}, u32[]{:S(2)}) copy-start(pred[8,129]{0,1:T(8,128)(4,1)} %constant.100) | copy-start | bytes 3100
  7.2 272.5 %all-reduce.6.cloned.1.call-start = ((), (), s32[]{:S(2)}) async-start(), calls=%async_computation | async-start | bytes 1572864 | tf_op jit(solution)/shard_map/psum | solution.py:134
  8.5 42.8 %collective-permute-start = (bf16[12,2,1024]{2,1,0:T(2,128)(2,1)S(1)}, bf16[12,2,1024]{2,1,0:T(2,128)(2,1)S(1)}, u32[]{:S(2)}, u32[]{:S(2)}) collective-permute-start(bf16[12,2,1024]{2,1,0:T(2,128)(2,1)S(1)} %get-tuple-element.26), channel_id=1, source_target_pairs={{0,8},{8,16},{16,24},{24,32},{32,40},{40,48},{48,56},{1,9},{9,17},... | collective-permute-start | bytes 147464 | tf_op jit(solution)/shard_map/ppermute | solution.py:22
  13.5 37.8 %collective-permute-start.1 = (bf16[12,2,1024]{2,1,0:T(2,128)(2,1)S(1)}, bf16[12,2,1024]{2,1,0:T(2,128)(2,1)S(1)}, u32[]{:S(2)}, u32[]{:S(2)}) collective-permute-start(bf16[12,2,1024]{2,1,0:T(2,128)(2,1)S(1)} %get-tuple-element.27), channel_id=1, source_target_pairs={{8,0},{16,8},{24,16},{32,24},{40,32},{48,40},{56,48},{9,1},{17,9},... | collective-permute-start | bytes 147464 | tf_op jit(solution)/shard_map/ppermute | solution.py:23
  57.3 7.4 copy-start.12
  69.6 38.6 %copy-start.4 = (f32[12,16,1024]{2,1,0:T(8,128)S(1)}, f32[12,16,1024]{2,1,0:T(8,128)}, u32[]{:S(2)}) copy-start(f32[12,16,1024]{2,1,0:T(8,128)} %param.11) | copy-start | bytes 2359300
  69.6 49.0 %copy-start.8 = (bf16[3,3,24,8]{2,3,1,0:T(8,128)(2,1)S(1)}, bf16[3,3,24,8]{2,3,1,0:T(8,128)(2,1)}, u32[]{:S(2)}) copy-start(bf16[3,3,24,8]{2,3,1,0:T(8,128)(2,1)} %param.16) | copy-start | bytes 10372
  108.2 28.8 %copy-start.3 = (bf16[12,16,1024]{2,1,0:T(8,128)(2,1)}, bf16[12,16,1024]{2,1,0:T(8,128)(2,1)S(1)}, u32[]{:S(2)}) copy-start(bf16[12,16,1024]{2,1,0:T(8,128)(2,1)S(1)} %all_gather.15) | copy-start | bytes 1179652
  110.3 26.7 %collective-permute-start.3 = (bf16[12,2,1024]{2,1,0:T(2,128)(2,1)S(1)}, bf16[12,2,1024]{2,1,0:T(2,128)(2,1)S(1)}, u32[]{:S(2)}, u32[]{:S(2)}) collective-permute-start(bf16[12,2,1024]{2,1,0:T(2,128)(2,1)S(1)} %get-tuple-element.25), channel_id=1, source_target_pairs={{8,0},{16,8},{24,16},{32,24},{40,32},{48,40},{56,48},{9,1},{17,9},... | collective-permute-start | bytes 147464 | tf_op jit(solution)/shard_map/ppermute | solution.py:23
  111.6 25.4 %collective-permute-start.2 = (bf16[12,2,1024]{2,1,0:T(2,128)(2,1)S(1)}, bf16[12,2,1024]{2,1,0:T(2,128)(2,1)S(1)}, u32[]{:S(2)}, u32[]{:S(2)}) collective-permute-start(bf16[12,2,1024]{2,1,0:T(2,128)(2,1)S(1)} %get-tuple-element.24), channel_id=1, source_target_pairs={{0,8},{8,16},{16,24},{24,32},{32,40},{40,48},{48,56},{1,9},{9,17},... | collective-permute-start | bytes 147464 | tf_op jit(solution)/shard_map/ppermute | solution.py:22
  182.0 18.4 %copy-start.13 = (bf16[3,3,8,12]{3,2,1,0:T(8,128)(2,1)S(1)}, bf16[3,3,8,12]{3,2,1,0:T(8,128)(2,1)}, u32[]{:S(2)}) copy-start(bf16[3,3,8,12]{3,2,1,0:T(8,128)(2,1)} %param.18) | copy-start | bytes 5188
  182.6 8.6 %collective-permute-start.5 = (bf16[8,1,1024]{2,0,1:T(8,128)(2,1)S(1)}, bf16[8,1,1024]{2,0,1:T(8,128)(2,1)S(1)}, u32[]{:S(2)}, u32[]{:S(2)}) collective-permute-start(bf16[8,1,1024]{2,0,1:T(8,128)(2,1)S(1)} %get-tuple-element.33), channel_id=1, source_target_pairs={{8,0},{16,8},{24,16},{32,24},{40,32},{48,40},{56,48},{9,1},{17,9},... | collective-permute-start | bytes 49160 | tf_op jit(solution)/shard_map/ppermute | solution.py:23
  183.9 8.7 %collective-permute-start.4 = (bf16[8,1,1024]{2,0,1:T(8,128)(2,1)S(1)}, bf16[8,1,1024]{2,0,1:T(8,128)(2,1)S(1)}, u32[]{:S(2)}, u32[]{:S(2)}) collective-permute-start(bf16[8,1,1024]{2,0,1:T(8,128)(2,1)S(1)} %get-tuple-element.32), channel_id=1, source_target_pairs={{0,8},{8,16},{16,24},{24,32},{32,40},{40,48},{48,56},{1,9},{9,17},... | collective-permute-start | bytes 49160 | tf_op jit(solution)/shard_map/ppermute | solution.py:22
  219.6 22.8 %copy-start.14 = (bf16[8]{0:T(256)(128)(2,1)S(1)}, bf16[8]{0:T(256)(128)(2,1)}, u32[]{:S(2)}) copy-start(bf16[8]{0:T(256)(128)(2,1)} %param.19) | copy-start | bytes 52
  222.7 121.6 %all-reduce.8.cloned.1.call-start = ((), (), s32[]{:S(2)}) async-start(), calls=%async_computation.1 | async-start | bytes 1572864 | tf_op jit(solution)/shard_map/psum | solution.py:134
  279.7 318.6 %all-gather.2.cloned.1.call-start = ((), (), s32[]{:S(2)}) async-start(), calls=%async_computation.2 | async-start | bytes 5013504 | tf_op jit(solution)/shard_map/all_gather | solution.py:149
  347.9 17.5 %collective-permute-start.7 = (bf16[12,1,1024]{2,1,0:T(2,128)(2,1)S(1)}, bf16[12,1,1024]{2,1,0:T(2,128)(2,1)S(1)}, u32[]{:S(2)}, u32[]{:S(2)}) collective-permute-start(bf16[12,1,1024]{2,1,0:T(2,128)(2,1)S(1)} %get-tuple-element.23), channel_id=1, source_target_pairs={{8,0},{16,8},{24,16},{32,24},{40,32},{48,40},{56,48},{9,1},{17,9},... | collective-permute-start | bytes 73736 | tf_op jit(solution)/shard_map/ppermute | solution.py:23
  349.2 16.2 %collective-permute-start.6 = (bf16[12,1,1024]{2,1,0:T(2,128)(2,1)S(1)}, bf16[12,1,1024]{2,1,0:T(2,128)(2,1)S(1)}, u32[]{:S(2)}, u32[]{:S(2)}) collective-permute-start(bf16[12,1,1024]{2,1,0:T(2,128)(2,1)S(1)} %get-tuple-element.22), channel_id=1, source_target_pairs={{0,8},{8,16},{16,24},{24,32},{32,40},{40,48},{48,56},{1,9},{9,17},... | collective-permute-start | bytes 73736 | tf_op jit(solution)/shard_map/ppermute | solution.py:22
  395.6 69.0 %collective-permute-start.9 = (bf16[8,1,1024]{2,0,1:T(8,128)(2,1)S(1)}, bf16[8,1,1024]{2,0,1:T(8,128)(2,1)S(1)}, u32[]{:S(2)}, u32[]{:S(2)}) collective-permute-start(bf16[8,1,1024]{2,0,1:T(8,128)(2,1)S(1)} %get-tuple-element.31), channel_id=1, source_target_pairs={{8,0},{16,8},{24,16},{32,24},{40,32},{48,40},{56,48},{9,1},{17,9},... | collective-permute-start | bytes 49160 | tf_op jit(solution)/shard_map/ppermute | solution.py:23
  396.9 67.7 %collective-permute-start.8 = (bf16[8,1,1024]{2,0,1:T(8,128)(2,1)S(1)}, bf16[8,1,1024]{2,0,1:T(8,128)(2,1)S(1)}, u32[]{:S(2)}, u32[]{:S(2)}) collective-permute-start(bf16[8,1,1024]{2,0,1:T(8,128)(2,1)S(1)} %get-tuple-element.30), channel_id=1, source_target_pairs={{0,8},{8,16},{16,24},{24,32},{32,40},{40,48},{48,56},{1,9},{9,17},... | collective-permute-start | bytes 49160 | tf_op jit(solution)/shard_map/ppermute | solution.py:22
  418.4 21.4 %copy-start.6 = (bf16[8,1,18,1024]{3,0,2,1:T(8,128)(2,1)S(1)}, bf16[8,1,18,1024]{3,0,2,1:T(8,128)(2,1)}, u32[]{:S(2)}) copy-start(bf16[8,1,18,1024]{3,0,2,1:T(8,128)(2,1)} %get-tuple-element.28) | copy-start | bytes 884740
  623.4 14.1 %copy-start.7 = (bf16[3,3,128,128]{2,3,1,0:T(8,128)(2,1)S(1)}, bf16[3,3,128,128]{2,3,1,0:T(8,128)(2,1)}, u32[]{:S(2)}) copy-start(bf16[3,3,128,128]{2,3,1,0:T(8,128)(2,1)} %all_gather.19) | copy-start | bytes 884740
  674.1 109.9 %copy-start.1 = (bf16[3,3,12,16]{3,2,1,0:T(8,128)(2,1)S(1)}, bf16[3,3,12,16]{3,2,1,0:T(8,128)(2,1)}, u32[]{:S(2)}) copy-start(bf16[3,3,12,16]{3,2,1,0:T(8,128)(2,1)} %param.14) | copy-start | bytes 10372
  (4 other events, 22.5 us)
Sparse Core Ops, SparseCore 0:
  222.9 42.4 all-reduce.5
  279.8 64.4 all-reduce.7
  465.5 38.5 all-gather.1
